TPU v7x, 32 devices: a whole 2x2x4 slice. The times are simulated.
32 devices in a mesh: gx: 8 (over z, x), gy: 4 (over y, core).
Axes of the slice: x: 2, y: 2, z: 4, core: 2. Of those that a mesh axis runs over, the one named last changes fastest.
Arguments:
- particles: float32 [4, 65536], P(None, ('gx', 'gy')), may hold values from -1 to 1, as said below
- tree_cells: float32 [10, 262144], P(None, ('gx', 'gy')), may hold values from -1 to 1, as said below
- let_list: int32 [32, 32, 4], P(('gx', 'gy')), may hold values from 0 to 63
- let_count: int32 [32, 32], P(('gx', 'gy')), may hold values from 1 to 4, as said below
- part_list: int32 [32, 4, 4], P(('gx', 'gy')), may hold values from 0 to 15
- cell_lists: int32 [512, 16], P(('gx', 'gy')), may hold values from 0 to 191
- near_lists: int32 [512, 8], P(('gx', 'gy')), may hold values from 0 to 31
Outputs:
- forces: float32 [4, 65536], P(None, ('gx', 'gy'))
Inputs may be any that keep to these rules, and one draw needn't show every extreme that they name: let_count is 4 wherever sender and receiver are at most 2 apart along gx+gy, and between 1 and 4 elsewhere. `particles`: positions lie in [-1, 1], masses are positive. `tree_cells`: centres lie in [-1, 1], masses are positive, the quadrupole is traceless.
All inputs are finite; a program needn't handle non-finite values.
Results may differ from a plain program's by a relative error of at most 0.0003.
Values sent between devices are 32-bit elements; how exact they have to be, the bound alone decides.
No kernel may reach another device: no remote copies, remote signals or barrier semaphores. Data moves between devices by JAX's collectives and lax.ppermute only.
A program may use at most 64 MiB of HBM per device.

v0:
```python
import jax
import jax.numpy as jnp
from jax import lax
from jax.sharding import PartitionSpec as P

BLK = 128


SOFTENING = 0.0025
near_offsets = (1, -1, 2, -2)


def from_behind(block, axis, distance):
    devices = range(lax.axis_size(axis))
    route = [(i - distance, i) for i in devices if i - distance in devices]
    return lax.ppermute(block, axis, route)


def cell_tile(targets, source):
    target_x = targets[0][:, None]
    target_y = targets[1][:, None]
    target_z = targets[2][:, None]
    delta_x = target_x - source[0][None, :]
    delta_y = target_y - source[1][None, :]
    delta_z = target_z - source[2][None, :]
    inverse = 1.0 / jnp.sqrt(delta_x * delta_x + delta_y * delta_y + delta_z * delta_z + SOFTENING)
    inv_square = inverse * inverse
    inv_cube = inverse * inv_square
    inv_five = inv_cube * inv_square
    masses = source[3][None, :]
    quad_x = (
        source[4][None, :] * delta_x + source[7][None, :] * delta_y + source[8][None, :] * delta_z
    )
    quad_y = (
        source[7][None, :] * delta_x + source[5][None, :] * delta_y + source[9][None, :] * delta_z
    )
    quad_z = (
        source[8][None, :] * delta_x + source[9][None, :] * delta_y + source[6][None, :] * delta_z
    )
    contracted = delta_x * quad_x + delta_y * quad_y + delta_z * quad_z
    radial = -masses * inv_cube - 2.5 * contracted * inv_five * inv_square
    accel_x = jnp.sum(radial * delta_x + quad_x * inv_five, axis=1)
    accel_y = jnp.sum(radial * delta_y + quad_y * inv_five, axis=1)
    accel_z = jnp.sum(radial * delta_z + quad_z * inv_five, axis=1)
    potential = jnp.sum(-masses * inverse - 0.5 * contracted * inv_five, axis=1)
    return jnp.stack([accel_x, accel_y, accel_z, potential])


def near_tile(targets, source):
    near_x = targets[0][:, None] - source[0][None, :]
    near_y = targets[1][:, None] - source[1][None, :]
    near_z = targets[2][:, None] - source[2][None, :]
    near_inverse = 1.0 / jnp.sqrt(near_x * near_x + near_y * near_y + near_z * near_z + SOFTENING)
    near_masses = source[3][None, :]
    near_radial = -near_masses * near_inverse * near_inverse * near_inverse
    accel_x = jnp.sum(near_radial * near_x, axis=1)
    accel_y = jnp.sum(near_radial * near_y, axis=1)
    accel_z = jnp.sum(near_radial * near_z, axis=1)
    potential = jnp.sum(-near_masses * near_inverse, axis=1)
    return jnp.stack([accel_x, accel_y, accel_z, potential])


def block_forces(target_blocks, cell_pool, near_pool, cell_lists, near_lists):
    cell_batch = jax.vmap(cell_tile)
    near_batch = jax.vmap(near_tile)

    def add_cells(total, column):
        return (total + cell_batch(target_blocks, cell_pool[column]), None)

    def add_near(total, column):
        return (total + near_batch(target_blocks, near_pool[column]), None)

    start = jnp.zeros(target_blocks.shape, jnp.float32)
    total, unused = lax.scan(add_cells, start, jnp.transpose(cell_lists))
    total, unused = lax.scan(add_near, total, jnp.transpose(near_lists))
    return total


def exchange_cells(chosen):
    moved = lax.all_to_all(chosen, ("gx", "gy"), split_axis=0, concat_axis=0, tiled=True)
    return moved


def body(particles, tree_cells, let_list, let_count, part_list, cell_lists, near_lists):
    part_blocks = jnp.transpose(particles.reshape(4, -1, BLK), (1, 0, 2))
    cell_blocks = jnp.transpose(tree_cells.reshape(10, -1, BLK), (1, 0, 2))
    peers = lax.axis_size(("gx", "gy"))
    slot_count = let_list.shape[2]
    live_mask = (
        lax.broadcasted_iota(jnp.int32, (peers, slot_count), 1) < let_count[0][:, None]
    ).astype(jnp.float32)
    chosen = cell_blocks[let_list[0]] * live_mask[:, :, None, None]
    received = exchange_cells(chosen).reshape(-1, 10, BLK)
    cell_pool = jnp.concatenate([cell_blocks, received], axis=0)
    near_parts = [part_blocks]
    for position, offset in enumerate(near_offsets):
        picked = part_blocks[part_list[0, position]]
        near_parts.append(from_behind(picked, ("gx", "gy"), offset))
    near_pool = jnp.concatenate(near_parts, axis=0)
    total = block_forces(part_blocks, cell_pool, near_pool, cell_lists, near_lists)
    return jnp.transpose(total, (1, 0, 2)).reshape(4, -1)


def solution(mesh):
    return jax.shard_map(
        body,
        mesh=mesh,
        in_specs=(
            P(None, ("gx", "gy")),
            P(None, ("gx", "gy")),
            P(("gx", "gy"), None, None),
            P(("gx", "gy"), None),
            P(("gx", "gy"), None, None),
            P(("gx", "gy"), None),
            P(("gx", "gy"), None),
        ),
        out_specs=P(None, ("gx", "gy")),
        check_vma=False,
    )
```

profile of v0, /device:TPU:0, one launch (start us, length us, event | category | flops | bytes accessed | tf_op | source)
XLA Modules:
  0.0 120.5 jit_solution(6718651355978896097)
XLA Ops:
  0.0 1.2 copy.51
  1.8 0.8 gather_fusion.2
  2.6 1.1 copy_multiply_fusion
  3.7 7.3 %all-to-all-start = ((f32[32,4,10,128]{3,1,2,0:T(4,128)}), f32[32,4,10,128]{3,1,2,0:T(4,128)S(1)}, u32[]{:S(2)}, u32[]{:S(2)}) async-start(f32[32,4,10,128]{3,1,2,0:T(4,128)} %copy_multiply_fusion), calls=%async_computation | async-start | bytes 1310720 | tf_op jit(solution)/shard_map/all_to_all | solution.py:80
  11.1 0.6 gather_fusion.3
  11.6 2.1 %collective-permute-start = (f32[4,4,128]{2,1,0:T(4,128)S(1)}, f32[4,4,128]{2,1,0:T(4,128)S(1)}, u32[]{:S(2)}, u32[]{:S(2)}) collective-permute-start(f32[4,4,128]{2,1,0:T(4,128)S(1)} %gather_fusion.3), channel_id=1, source_target_pairs={{0,1},{1,2},{2,3},{3,4},{4,5},{5,6},{6,7},{7,8},{8,9},{9,10},{10,1... | collective-permute-start | bytes 24584 | tf_op jit(solution)/shard_map/ppermute | solution.py:16
  13.8 0.6 gather_fusion.4
  14.4 1.3 %collective-permute-start.1 = (f32[4,4,128]{2,1,0:T(4,128)S(1)}, f32[4,4,128]{2,1,0:T(4,128)S(1)}, u32[]{:S(2)}, u32[]{:S(2)}) collective-permute-start(f32[4,4,128]{2,1,0:T(4,128)S(1)} %gather_fusion.4), channel_id=1, source_target_pairs={{1,0},{2,1},{3,2},{4,3},{5,4},{6,5},{7,6},{8,7},{9,8},{10,9},{11,1... | collective-permute-start | bytes 24584 | tf_op jit(solution)/shard_map/ppermute | solution.py:16
  15.7 0.6 gather_fusion.5
  16.3 5.8 %collective-permute-start.2 = (f32[4,4,128]{2,1,0:T(4,128)S(1)}, f32[4,4,128]{2,1,0:T(4,128)S(1)}, u32[]{:S(2)}, u32[]{:S(2)}) collective-permute-start(f32[4,4,128]{2,1,0:T(4,128)S(1)} %gather_fusion.5), channel_id=1, source_target_pairs={{0,2},{1,3},{2,4},{3,5},{4,6},{5,7},{6,8},{7,9},{8,10},{9,11},{10,... | collective-permute-start | bytes 24584 | tf_op jit(solution)/shard_map/ppermute | solution.py:16
  22.1 0.6 gather_fusion.6
  22.6 1.3 %collective-permute-start.3 = (f32[4,4,128]{2,1,0:T(4,128)S(1)}, f32[4,4,128]{2,1,0:T(4,128)S(1)}, u32[]{:S(2)}, u32[]{:S(2)}) collective-permute-start(f32[4,4,128]{2,1,0:T(4,128)S(1)} %gather_fusion.6), channel_id=1, source_target_pairs={{2,0},{3,1},{4,2},{5,3},{6,4},{7,5},{8,6},{9,7},{10,8},{11,9},{12,... | collective-permute-start | bytes 24584 | tf_op jit(solution)/shard_map/ppermute | solution.py:16
  24.1 4.5 %collective-permute-done.3 = f32[4,4,128]{2,1,0:T(4,128)S(1)} collective-permute-done((f32[4,4,128]{2,1,0:T(4,128)S(1)}, f32[4,4,128]{2,1,0:T(4,128)S(1)}, u32[]{:S(2)}, u32[]{:S(2)}) %collective-permute-start.3) | collective-permute-done | bytes 8224 | tf_op jit(solution)/shard_map/ppermute | solution.py:16
  29.1 0.6 copy.47
  29.8 61.0 %while.22 = (s32[]{:T(128)}, f32[16,4,128]{2,0,1:T(8,128)S(1)}, s32[16,16]{1,0:T(8,128)S(1)}, f32[192,10,128]{2,1,0:T(8,128)S(1)}, f32[16,4,128]{2,0,1:T(8,128)S(1)}, /*index=5*/s32[]{:T(128)}, s32[]{:T(128)}) while((s32[]{:T(128)}, f32[16,4,128]{2,0,1:T(8,128)S(1)}, s32[16,16]{1,0:T(8,128)S(1)}, f32[192,10,128]{2,1,0:T(8,128)S(1)}, ...), condition=%wide.region_5.6_spmd.clone, body=%wide.region_0.5_spmd.clone.sunk | while | flops 14191667 | bytes 618851 | solution.py:74
  29.8 0.6 gather_fusion.1
  30.5 3.1 %fusion.52 = (f32[16,128]{1,0:T(8,128)S(1)}, f32[16,128]{1,0:T(8,128)S(1)}, f32[16,128]{1,0:T(8,128)S(1)}, f32[16,128]{1,0:T(8,128)S(1)}) fusion(f32[16,128]{1,0:T(8,128)S(1)} %bitcast.170, f32[16,128]{1,0:T(8,128)S(1)} %bitcast.171, f32[16,128]{1,0:T(8,128)S(1)} %bitcast.172, f32[16,128]{1,0:T(8,128)S(1)} %bitcast.173, ...), kind=kLoop, calls=%fused_computation.67.clone.1 | loop fusion | flops 14147584 | bytes 139264 | tf_op jit(solution)/shard_map/while/body/eval_jaxpr/vmap()/reduce_sum | solution.py:42
  33.6 0.6 gather_fusion.1
  34.3 3.1 %fusion.52 = (f32[16,128]{1,0:T(8,128)S(1)}, f32[16,128]{1,0:T(8,128)S(1)}, f32[16,128]{1,0:T(8,128)S(1)}, f32[16,128]{1,0:T(8,128)S(1)}) fusion(f32[16,128]{1,0:T(8,128)S(1)} %bitcast.170, f32[16,128]{1,0:T(8,128)S(1)} %bitcast.171, f32[16,128]{1,0:T(8,128)S(1)} %bitcast.172, f32[16,128]{1,0:T(8,128)S(1)} %bitcast.173, ...), kind=kLoop, calls=%fused_computation.67.clone.1 | loop fusion | flops 14147584 | bytes 139264 | tf_op jit(solution)/shard_map/while/body/eval_jaxpr/vmap()/reduce_sum | solution.py:42
  37.4 0.6 gather_fusion.1
  38.1 3.1 %fusion.52 = (f32[16,128]{1,0:T(8,128)S(1)}, f32[16,128]{1,0:T(8,128)S(1)}, f32[16,128]{1,0:T(8,128)S(1)}, f32[16,128]{1,0:T(8,128)S(1)}) fusion(f32[16,128]{1,0:T(8,128)S(1)} %bitcast.170, f32[16,128]{1,0:T(8,128)S(1)} %bitcast.171, f32[16,128]{1,0:T(8,128)S(1)} %bitcast.172, f32[16,128]{1,0:T(8,128)S(1)} %bitcast.173, ...), kind=kLoop, calls=%fused_computation.67.clone.1 | loop fusion | flops 14147584 | bytes 139264 | tf_op jit(solution)/shard_map/while/body/eval_jaxpr/vmap()/reduce_sum | solution.py:42
  41.2 0.6 gather_fusion.1
  41.9 3.1 %fusion.52 = (f32[16,128]{1,0:T(8,128)S(1)}, f32[16,128]{1,0:T(8,128)S(1)}, f32[16,128]{1,0:T(8,128)S(1)}, f32[16,128]{1,0:T(8,128)S(1)}) fusion(f32[16,128]{1,0:T(8,128)S(1)} %bitcast.170, f32[16,128]{1,0:T(8,128)S(1)} %bitcast.171, f32[16,128]{1,0:T(8,128)S(1)} %bitcast.172, f32[16,128]{1,0:T(8,128)S(1)} %bitcast.173, ...), kind=kLoop, calls=%fused_computation.67.clone.1 | loop fusion | flops 14147584 | bytes 139264 | tf_op jit(solution)/shard_map/while/body/eval_jaxpr/vmap()/reduce_sum | solution.py:42
  45.1 0.6 gather_fusion.1
  45.7 3.1 %fusion.52 = (f32[16,128]{1,0:T(8,128)S(1)}, f32[16,128]{1,0:T(8,128)S(1)}, f32[16,128]{1,0:T(8,128)S(1)}, f32[16,128]{1,0:T(8,128)S(1)}) fusion(f32[16,128]{1,0:T(8,128)S(1)} %bitcast.170, f32[16,128]{1,0:T(8,128)S(1)} %bitcast.171, f32[16,128]{1,0:T(8,128)S(1)} %bitcast.172, f32[16,128]{1,0:T(8,128)S(1)} %bitcast.173, ...), kind=kLoop, calls=%fused_computation.67.clone.1 | loop fusion | flops 14147584 | bytes 139264 | tf_op jit(solution)/shard_map/while/body/eval_jaxpr/vmap()/reduce_sum | solution.py:42
  48.9 0.6 gather_fusion.1
  49.5 3.1 %fusion.52 = (f32[16,128]{1,0:T(8,128)S(1)}, f32[16,128]{1,0:T(8,128)S(1)}, f32[16,128]{1,0:T(8,128)S(1)}, f32[16,128]{1,0:T(8,128)S(1)}) fusion(f32[16,128]{1,0:T(8,128)S(1)} %bitcast.170, f32[16,128]{1,0:T(8,128)S(1)} %bitcast.171, f32[16,128]{1,0:T(8,128)S(1)} %bitcast.172, f32[16,128]{1,0:T(8,128)S(1)} %bitcast.173, ...), kind=kLoop, calls=%fused_computation.67.clone.1 | loop fusion | flops 14147584 | bytes 139264 | tf_op jit(solution)/shard_map/while/body/eval_jaxpr/vmap()/reduce_sum | solution.py:42
  53.3 3.1 %fusion.52 = (f32[16,128]{1,0:T(8,128)S(1)}, f32[16,128]{1,0:T(8,128)S(1)}, f32[16,128]{1,0:T(8,128)S(1)}, f32[16,128]{1,0:T(8,128)S(1)}) fusion(f32[16,128]{1,0:T(8,128)S(1)} %bitcast.170, f32[16,128]{1,0:T(8,128)S(1)} %bitcast.171, f32[16,128]{1,0:T(8,128)S(1)} %bitcast.172, f32[16,128]{1,0:T(8,128)S(1)} %bitcast.173, ...), kind=kLoop, calls=%fused_computation.67.clone.1 | loop fusion | flops 14147584 | bytes 139264 | tf_op jit(solution)/shard_map/while/body/eval_jaxpr/vmap()/reduce_sum | solution.py:42
  57.2 3.1 %fusion.52 = (f32[16,128]{1,0:T(8,128)S(1)}, f32[16,128]{1,0:T(8,128)S(1)}, f32[16,128]{1,0:T(8,128)S(1)}, f32[16,128]{1,0:T(8,128)S(1)}) fusion(f32[16,128]{1,0:T(8,128)S(1)} %bitcast.170, f32[16,128]{1,0:T(8,128)S(1)} %bitcast.171, f32[16,128]{1,0:T(8,128)S(1)} %bitcast.172, f32[16,128]{1,0:T(8,128)S(1)} %bitcast.173, ...), kind=kLoop, calls=%fused_computation.67.clone.1 | loop fusion | flops 14147584 | bytes 139264 | tf_op jit(solution)/shard_map/while/body/eval_jaxpr/vmap()/reduce_sum | solution.py:42
  61.0 3.1 %fusion.52 = (f32[16,128]{1,0:T(8,128)S(1)}, f32[16,128]{1,0:T(8,128)S(1)}, f32[16,128]{1,0:T(8,128)S(1)}, f32[16,128]{1,0:T(8,128)S(1)}) fusion(f32[16,128]{1,0:T(8,128)S(1)} %bitcast.170, f32[16,128]{1,0:T(8,128)S(1)} %bitcast.171, f32[16,128]{1,0:T(8,128)S(1)} %bitcast.172, f32[16,128]{1,0:T(8,128)S(1)} %bitcast.173, ...), kind=kLoop, calls=%fused_computation.67.clone.1 | loop fusion | flops 14147584 | bytes 139264 | tf_op jit(solution)/shard_map/while/body/eval_jaxpr/vmap()/reduce_sum | solution.py:42
  64.8 3.1 %fusion.52 = (f32[16,128]{1,0:T(8,128)S(1)}, f32[16,128]{1,0:T(8,128)S(1)}, f32[16,128]{1,0:T(8,128)S(1)}, f32[16,128]{1,0:T(8,128)S(1)}) fusion(f32[16,128]{1,0:T(8,128)S(1)} %bitcast.170, f32[16,128]{1,0:T(8,128)S(1)} %bitcast.171, f32[16,128]{1,0:T(8,128)S(1)} %bitcast.172, f32[16,128]{1,0:T(8,128)S(1)} %bitcast.173, ...), kind=kLoop, calls=%fused_computation.67.clone.1 | loop fusion | flops 14147584 | bytes 139264 | tf_op jit(solution)/shard_map/while/body/eval_jaxpr/vmap()/reduce_sum | solution.py:42
  68.0 0.6 gather_fusion.1
  68.6 3.1 %fusion.52 = (f32[16,128]{1,0:T(8,128)S(1)}, f32[16,128]{1,0:T(8,128)S(1)}, f32[16,128]{1,0:T(8,128)S(1)}, f32[16,128]{1,0:T(8,128)S(1)}) fusion(f32[16,128]{1,0:T(8,128)S(1)} %bitcast.170, f32[16,128]{1,0:T(8,128)S(1)} %bitcast.171, f32[16,128]{1,0:T(8,128)S(1)} %bitcast.172, f32[16,128]{1,0:T(8,128)S(1)} %bitcast.173, ...), kind=kLoop, calls=%fused_computation.67.clone.1 | loop fusion | flops 14147584 | bytes 139264 | tf_op jit(solution)/shard_map/while/body/eval_jaxpr/vmap()/reduce_sum | solution.py:42
  72.4 3.1 %fusion.52 = (f32[16,128]{1,0:T(8,128)S(1)}, f32[16,128]{1,0:T(8,128)S(1)}, f32[16,128]{1,0:T(8,128)S(1)}, f32[16,128]{1,0:T(8,128)S(1)}) fusion(f32[16,128]{1,0:T(8,128)S(1)} %bitcast.170, f32[16,128]{1,0:T(8,128)S(1)} %bitcast.171, f32[16,128]{1,0:T(8,128)S(1)} %bitcast.172, f32[16,128]{1,0:T(8,128)S(1)} %bitcast.173, ...), kind=kLoop, calls=%fused_computation.67.clone.1 | loop fusion | flops 14147584 | bytes 139264 | tf_op jit(solution)/shard_map/while/body/eval_jaxpr/vmap()/reduce_sum | solution.py:42
  76.2 3.1 %fusion.52 = (f32[16,128]{1,0:T(8,128)S(1)}, f32[16,128]{1,0:T(8,128)S(1)}, f32[16,128]{1,0:T(8,128)S(1)}, f32[16,128]{1,0:T(8,128)S(1)}) fusion(f32[16,128]{1,0:T(8,128)S(1)} %bitcast.170, f32[16,128]{1,0:T(8,128)S(1)} %bitcast.171, f32[16,128]{1,0:T(8,128)S(1)} %bitcast.172, f32[16,128]{1,0:T(8,128)S(1)} %bitcast.173, ...), kind=kLoop, calls=%fused_computation.67.clone.1 | loop fusion | flops 14147584 | bytes 139264 | tf_op jit(solution)/shard_map/while/body/eval_jaxpr/vmap()/reduce_sum | solution.py:42
  80.0 3.1 %fusion.52 = (f32[16,128]{1,0:T(8,128)S(1)}, f32[16,128]{1,0:T(8,128)S(1)}, f32[16,128]{1,0:T(8,128)S(1)}, f32[16,128]{1,0:T(8,128)S(1)}) fusion(f32[16,128]{1,0:T(8,128)S(1)} %bitcast.170, f32[16,128]{1,0:T(8,128)S(1)} %bitcast.171, f32[16,128]{1,0:T(8,128)S(1)} %bitcast.172, f32[16,128]{1,0:T(8,128)S(1)} %bitcast.173, ...), kind=kLoop, calls=%fused_computation.67.clone.1 | loop fusion | flops 14147584 | bytes 139264 | tf_op jit(solution)/shard_map/while/body/eval_jaxpr/vmap()/reduce_sum | solution.py:42
  83.9 3.1 %fusion.52 = (f32[16,128]{1,0:T(8,128)S(1)}, f32[16,128]{1,0:T(8,128)S(1)}, f32[16,128]{1,0:T(8,128)S(1)}, f32[16,128]{1,0:T(8,128)S(1)}) fusion(f32[16,128]{1,0:T(8,128)S(1)} %bitcast.170, f32[16,128]{1,0:T(8,128)S(1)} %bitcast.171, f32[16,128]{1,0:T(8,128)S(1)} %bitcast.172, f32[16,128]{1,0:T(8,128)S(1)} %bitcast.173, ...), kind=kLoop, calls=%fused_computation.67.clone.1 | loop fusion | flops 14147584 | bytes 139264 | tf_op jit(solution)/shard_map/while/body/eval_jaxpr/vmap()/reduce_sum | solution.py:42
  87.7 3.1 %fusion.52 = (f32[16,128]{1,0:T(8,128)S(1)}, f32[16,128]{1,0:T(8,128)S(1)}, f32[16,128]{1,0:T(8,128)S(1)}, f32[16,128]{1,0:T(8,128)S(1)}) fusion(f32[16,128]{1,0:T(8,128)S(1)} %bitcast.170, f32[16,128]{1,0:T(8,128)S(1)} %bitcast.171, f32[16,128]{1,0:T(8,128)S(1)} %bitcast.172, f32[16,128]{1,0:T(8,128)S(1)} %bitcast.173, ...), kind=kLoop, calls=%fused_computation.67.clone.1 | loop fusion | flops 14147584 | bytes 139264 | tf_op jit(solution)/shard_map/while/body/eval_jaxpr/vmap()/reduce_sum | solution.py:42
  90.8 29.0 %while.21 = (s32[]{:T(128)}, f32[16,4,128]{2,0,1:T(8,128)S(1)}, f32[16,4,128]{2,0,1:T(8,128)S(1)}, s32[8,16]{1,0:T(8,128)}, f32[32,4,128]{2,1,0:T(4,128)S(1)}, /*index=5*/s32[]{:T(128)}) while((s32[]{:T(128)}, f32[16,4,128]{2,0,1:T(8,128)S(1)}, f32[16,4,128]{2,0,1:T(8,128)S(1)}, s32[8,16]{1,0:T(8,128)}, f32[32,4,128]{2,1,0:T(4,128)S(1)}, ...), condition=%wide.region_11.12_spmd, body=%wide.region_6.11_spmd.sunk | while | flops 5008434 | bytes 373073 | solution.py:75
  90.8 0.7 fusion.47
  91.5 0.6 gather_fusion
  92.2 2.2 %fusion.49 = (f32[16,128]{1,0:T(8,128)S(1)}, f32[16,128]{1,0:T(8,128)S(1)}, f32[16,128]{1,0:T(8,128)S(1)}, f32[16,128]{1,0:T(8,128)S(1)}) fusion(f32[16,128]{1,0:T(8,128)S(1)} %bitcast.183, f32[16,128]{1,0:T(8,128)S(1)} %get-tuple-element.244, f32[16,128]{1,0:T(8,128)S(1)} %bitcast.184, f32[16,128]{1,0:T(8,128)S(1)} %bitcast.182, ...), kind=kLoop, calls=%fused_computation.19.clone.1 | loop fusion | flops 4972544 | bytes 90112 | tf_op jit(solution)/shard_map/while/body/eval_jaxpr/vmap()/reduce_sum | solution.py:56
  94.4 0.7 fusion.47
  95.1 0.6 gather_fusion
  95.8 2.2 %fusion.49 = (f32[16,128]{1,0:T(8,128)S(1)}, f32[16,128]{1,0:T(8,128)S(1)}, f32[16,128]{1,0:T(8,128)S(1)}, f32[16,128]{1,0:T(8,128)S(1)}) fusion(f32[16,128]{1,0:T(8,128)S(1)} %bitcast.183, f32[16,128]{1,0:T(8,128)S(1)} %get-tuple-element.244, f32[16,128]{1,0:T(8,128)S(1)} %bitcast.184, f32[16,128]{1,0:T(8,128)S(1)} %bitcast.182, ...), kind=kLoop, calls=%fused_computation.19.clone.1 | loop fusion | flops 4972544 | bytes 90112 | tf_op jit(solution)/shard_map/while/body/eval_jaxpr/vmap()/reduce_sum | solution.py:56
  98.1 0.7 fusion.47
  98.8 0.6 gather_fusion
  99.4 2.2 %fusion.49 = (f32[16,128]{1,0:T(8,128)S(1)}, f32[16,128]{1,0:T(8,128)S(1)}, f32[16,128]{1,0:T(8,128)S(1)}, f32[16,128]{1,0:T(8,128)S(1)}) fusion(f32[16,128]{1,0:T(8,128)S(1)} %bitcast.183, f32[16,128]{1,0:T(8,128)S(1)} %get-tuple-element.244, f32[16,128]{1,0:T(8,128)S(1)} %bitcast.184, f32[16,128]{1,0:T(8,128)S(1)} %bitcast.182, ...), kind=kLoop, calls=%fused_computation.19.clone.1 | loop fusion | flops 4972544 | bytes 90112 | tf_op jit(solution)/shard_map/while/body/eval_jaxpr/vmap()/reduce_sum | solution.py:56
  101.7 0.7 fusion.47
  102.4 0.6 gather_fusion
  103.0 2.2 %fusion.49 = (f32[16,128]{1,0:T(8,128)S(1)}, f32[16,128]{1,0:T(8,128)S(1)}, f32[16,128]{1,0:T(8,128)S(1)}, f32[16,128]{1,0:T(8,128)S(1)}) fusion(f32[16,128]{1,0:T(8,128)S(1)} %bitcast.183, f32[16,128]{1,0:T(8,128)S(1)} %get-tuple-element.244, f32[16,128]{1,0:T(8,128)S(1)} %bitcast.184, f32[16,128]{1,0:T(8,128)S(1)} %bitcast.182, ...), kind=kLoop, calls=%fused_computation.19.clone.1 | loop fusion | flops 4972544 | bytes 90112 | tf_op jit(solution)/shard_map/while/body/eval_jaxpr/vmap()/reduce_sum | solution.py:56
  105.3 0.7 fusion.47
  106.0 0.6 gather_fusion
  106.7 2.2 %fusion.49 = (f32[16,128]{1,0:T(8,128)S(1)}, f32[16,128]{1,0:T(8,128)S(1)}, f32[16,128]{1,0:T(8,128)S(1)}, f32[16,128]{1,0:T(8,128)S(1)}) fusion(f32[16,128]{1,0:T(8,128)S(1)} %bitcast.183, f32[16,128]{1,0:T(8,128)S(1)} %get-tuple-element.244, f32[16,128]{1,0:T(8,128)S(1)} %bitcast.184, f32[16,128]{1,0:T(8,128)S(1)} %bitcast.182, ...), kind=kLoop, calls=%fused_computation.19.clone.1 | loop fusion | flops 4972544 | bytes 90112 | tf_op jit(solution)/shard_map/while/body/eval_jaxpr/vmap()/reduce_sum | solution.py:56
  108.9 0.7 fusion.47
  109.7 0.6 gather_fusion
  110.3 2.2 %fusion.49 = (f32[16,128]{1,0:T(8,128)S(1)}, f32[16,128]{1,0:T(8,128)S(1)}, f32[16,128]{1,0:T(8,128)S(1)}, f32[16,128]{1,0:T(8,128)S(1)}) fusion(f32[16,128]{1,0:T(8,128)S(1)} %bitcast.183, f32[16,128]{1,0:T(8,128)S(1)} %get-tuple-element.244, f32[16,128]{1,0:T(8,128)S(1)} %bitcast.184, f32[16,128]{1,0:T(8,128)S(1)} %bitcast.182, ...), kind=kLoop, calls=%fused_computation.19.clone.1 | loop fusion | flops 4972544 | bytes 90112 | tf_op jit(solution)/shard_map/while/body/eval_jaxpr/vmap()/reduce_sum | solution.py:56
  112.6 0.7 fusion.47
  113.3 0.6 gather_fusion
  113.9 2.2 %fusion.49 = (f32[16,128]{1,0:T(8,128)S(1)}, f32[16,128]{1,0:T(8,128)S(1)}, f32[16,128]{1,0:T(8,128)S(1)}, f32[16,128]{1,0:T(8,128)S(1)}) fusion(f32[16,128]{1,0:T(8,128)S(1)} %bitcast.183, f32[16,128]{1,0:T(8,128)S(1)} %get-tuple-element.244, f32[16,128]{1,0:T(8,128)S(1)} %bitcast.184, f32[16,128]{1,0:T(8,128)S(1)} %bitcast.182, ...), kind=kLoop, calls=%fused_computation.19.clone.1 | loop fusion | flops 4972544 | bytes 90112 | tf_op jit(solution)/shard_map/while/body/eval_jaxpr/vmap()/reduce_sum | solution.py:56
  116.2 0.7 fusion.47
  116.9 0.6 gather_fusion
  117.5 2.2 %fusion.49 = (f32[16,128]{1,0:T(8,128)S(1)}, f32[16,128]{1,0:T(8,128)S(1)}, f32[16,128]{1,0:T(8,128)S(1)}, f32[16,128]{1,0:T(8,128)S(1)}) fusion(f32[16,128]{1,0:T(8,128)S(1)} %bitcast.183, f32[16,128]{1,0:T(8,128)S(1)} %get-tuple-element.244, f32[16,128]{1,0:T(8,128)S(1)} %bitcast.184, f32[16,128]{1,0:T(8,128)S(1)} %bitcast.182, ...), kind=kLoop, calls=%fused_computation.19.clone.1 | loop fusion | flops 4972544 | bytes 90112 | tf_op jit(solution)/shard_map/while/body/eval_jaxpr/vmap()/reduce_sum | solution.py:56
  119.8 0.6 copy.57
  (157 shorter events, 8.2 us)
Async XLA Ops:
  0.0 1.4 %copy-start.2 = (s32[1,32,4]{1,2,0:T(4,128)S(1)}, s32[1,32,4]{1,2,0:T(4,128)}, u32[]{:S(2)}) copy-start(s32[1,32,4]{1,2,0:T(4,128)} %param.13) | copy-start | bytes 1540
  0.0 1.7 %copy-start.4 = (s32[1,32]{1,0:T(1,128)S(1)}, s32[1,32]{1,0:T(1,128)}, u32[]{:S(2)}) copy-start(s32[1,32]{1,0:T(1,128)} %param.14) | copy-start | bytes 388
  2.5 8.5 %copy-start.3 = (s32[1,4,4]{2,1,0:T(4,128)S(1)}, s32[1,4,4]{2,1,0:T(4,128)}, u32[]{:S(2)}) copy-start(s32[1,4,4]{2,1,0:T(4,128)} %param.15) | copy-start | bytes 196
  2.5 8.5 %copy-start = (f32[4,2048]{1,0:T(4,128)S(1)}, f32[4,2048]{1,0:T(4,128)}, u32[]{:S(2)}) copy-start(f32[4,2048]{1,0:T(4,128)} %param.11) | copy-start | bytes 98308
  2.5 21.4 %copy-start.1 = (s32[16,16]{1,0:T(8,128)S(1)}, s32[16,16]{1,0:T(8,128)}, u32[]{:S(2)}) copy-start(s32[16,16]{1,0:T(8,128)} %param.16) | copy-start | bytes 3076
  3.7 25.2 %all-to-all-start = ((f32[32,4,10,128]{3,1,2,0:T(4,128)}), f32[32,4,10,128]{3,1,2,0:T(4,128)S(1)}, u32[]{:S(2)}, u32[]{:S(2)}) async-start(f32[32,4,10,128]{3,1,2,0:T(4,128)} %copy_multiply_fusion), calls=%async_computation | async-start | bytes 1310720 | tf_op jit(solution)/shard_map/all_to_all | solution.py:80
  11.6 12.4 %collective-permute-start = (f32[4,4,128]{2,1,0:T(4,128)S(1)}, f32[4,4,128]{2,1,0:T(4,128)S(1)}, u32[]{:S(2)}, u32[]{:S(2)}) collective-permute-start(f32[4,4,128]{2,1,0:T(4,128)S(1)} %gather_fusion.3), channel_id=1, source_target_pairs={{0,1},{1,2},{2,3},{3,4},{4,5},{5,6},{6,7},{7,8},{8,9},{9,10},{10,1... | collective-permute-start | bytes 24584 | tf_op jit(solution)/shard_map/ppermute | solution.py:16
  14.4 9.7 %collective-permute-start.1 = (f32[4,4,128]{2,1,0:T(4,128)S(1)}, f32[4,4,128]{2,1,0:T(4,128)S(1)}, u32[]{:S(2)}, u32[]{:S(2)}) collective-permute-start(f32[4,4,128]{2,1,0:T(4,128)S(1)} %gather_fusion.4), channel_id=1, source_target_pairs={{1,0},{2,1},{3,2},{4,3},{5,4},{6,5},{7,6},{8,7},{9,8},{10,9},{11,1... | collective-permute-start | bytes 24584 | tf_op jit(solution)/shard_map/ppermute | solution.py:16
  16.3 7.8 %collective-permute-start.2 = (f32[4,4,128]{2,1,0:T(4,128)S(1)}, f32[4,4,128]{2,1,0:T(4,128)S(1)}, u32[]{:S(2)}, u32[]{:S(2)}) collective-permute-start(f32[4,4,128]{2,1,0:T(4,128)S(1)} %gather_fusion.5), channel_id=1, source_target_pairs={{0,2},{1,3},{2,4},{3,5},{4,6},{5,7},{6,8},{7,9},{8,10},{9,11},{10,... | collective-permute-start | bytes 24584 | tf_op jit(solution)/shard_map/ppermute | solution.py:16
  22.6 5.9 %collective-permute-start.3 = (f32[4,4,128]{2,1,0:T(4,128)S(1)}, f32[4,4,128]{2,1,0:T(4,128)S(1)}, u32[]{:S(2)}, u32[]{:S(2)}) collective-permute-start(f32[4,4,128]{2,1,0:T(4,128)S(1)} %gather_fusion.6), channel_id=1, source_target_pairs={{2,0},{3,1},{4,2},{5,3},{6,4},{7,5},{8,6},{9,7},{10,8},{11,9},{12,... | collective-permute-start | bytes 24584 | tf_op jit(solution)/shard_map/ppermute | solution.py:16
where the time goes:
time: 122 us; the launch traced here: 120 us
  other arithmetic  76 us (62%)
  local copies, waits for them, and re-layouts  20 us (16%)
  starting transfers between devices  17.8 us (15%)
  waiting for transfers between devices  4.84 us (4%)
  loops' own time  1.53 us (1%)
    reduce_sum x16, other arithmetic, cell_tile(): accel_x = jnp.sum(radial * delta_x + quad_x * inv_five, axis=1)  49.4 us
    reduce_sum x8, other arithmetic, near_tile(): accel_x = jnp.sum(near_radial * near_x, axis=1)  18 us
    ppermute x4, starting transfers between devices, from_behind(): return lax.ppermute(block, axis, route)  10.5 us
    gather x16, local copies, waits for them, and re-layouts, add_cells(): return (total + cell_batch(target_blocks, cell_pool[column]), None)  9.04 us
    all_to_all x1, starting transfers between devices, exchange_cells(): lax.all_to_all(chosen, ('gx', 'gy'), split_axis=0, concat_axis=0, tiled=T...  7.3 us
    select_n x8, other arithmetic, add_near(): return (total + near_batch(target_blocks, near_pool[column]), None)  5.58 us
    gather x8, local copies, waits for them, and re-layouts, add_near(): return (total + near_batch(target_blocks, near_pool[column]), None)  4.69 us
    ppermute x4, waiting for transfers between devices, from_behind(): return lax.ppermute(block, axis, route)  4.46 us
  transfers between devices with their start and end apart: 5, of which 2 were waited for; matrix products, arithmetic and copies ran while one was open for 2% of the time, Pallas kernels for 0%

commit v1 on v0

v1 whole, which is shorter than its diff:
```python
import functools

import jax
import jax.numpy as jnp
from jax import lax
from jax.experimental import pallas as pl
from jax.experimental.pallas import tpu as pltpu
from jax.sharding import PartitionSpec as P

BLK = 128
ROWS = 16
KEEP = (0, 1, 2, 3, 4, 5, 7, 8, 9)

SOFTENING = 0.0025
near_offsets = (1, -1, 2, -2)
F32 = jnp.float32
B16 = jnp.bfloat16


def from_behind(block, axis, distance):
    devices = range(lax.axis_size(axis))
    route = [(i - distance, i) for i in devices if i - distance in devices]
    return lax.ppermute(block, axis, route)


def split3(value):
    high = value.astype(B16)
    rest = value - high.astype(F32)
    middle = rest.astype(B16)
    low = (rest - middle.astype(F32)).astype(B16)
    return high, middle, low


def split2(value):
    high = value.astype(B16)
    return high, (value - high.astype(F32)).astype(B16)


def stack_rows(rows):
    sub = lax.broadcasted_iota(jnp.int32, (8, BLK), 0)
    out = rows[0]
    for i in range(1, len(rows)):
        if rows[i] is not None:
            out = jnp.where(sub == i, rows[i], out)
    return out


def wide(row):
    return jnp.broadcast_to(row, (8, BLK))


def distance_rows(x, y, z):
    square = x * x + y * y + z * z + SOFTENING
    zero = jnp.zeros((8, BLK), F32)
    one = jnp.where(lax.broadcasted_iota(jnp.int32, (8, BLK), 0) == 2, 1.0, 0.0)
    return jnp.concatenate([stack_rows([x, y, z, square, zero, zero, zero, zero]), one], axis=0)


def quadrupole_rows(x, y, z, xx, yy, xy, xz, yz):
    xx, yy, xy, xz, yz = (2.5 * v for v in (xx, yy, xy, xz, yz))
    zz = -(xx + yy)
    qx = xx * x + xy * y + xz * z
    qy = xy * x + yy * y + yz * z
    qz = xz * x + yz * y + zz * z
    inner = qx * x + qy * y + qz * z
    zero = jnp.zeros((8, BLK), F32)
    first = stack_rows([qx, qy, qz, inner, xx, yy, zz, xy])
    second = stack_rows([xz, yz, zero, zero, zero, zero, zero, zero])
    return jnp.concatenate([first, second], axis=0)


def target_rows(x, y, z):
    one = jnp.ones((8, BLK), F32)
    zero = jnp.zeros((8, BLK), F32)
    first = stack_rows([-2 * x, -2 * y, -2 * z, one, x * x, y * y, z * z, 2 * x * y])
    second = stack_rows([2 * x * z, 2 * y * z, x * x + y * y + z * z, zero, zero, zero, zero, zero])
    return jnp.concatenate([first, second], axis=0)


def store_source(slot, weights, rows):
    high, middle, low = split3(rows)
    weights[slot, 0:ROWS] = high
    weights[slot, ROWS : 2 * ROWS] = middle
    weights[slot, 2 * ROWS :] = low


def six(weights):
    high, middle, low = weights[0:ROWS], weights[ROWS : 2 * ROWS], weights[2 * ROWS :]
    return jnp.concatenate([high, high, high, middle, middle, low], axis=0)


def contract(left, right):
    return lax.dot_general(left, right, (((1,), (1,)), ((), ())), preferred_element_type=F32)


def cell_pair(targets, weights, masses):
    both = jnp.dot(targets, six(weights), preferred_element_type=F32)
    inverse = lax.rsqrt(both[:, :BLK])
    square = inverse * inverse
    fifth = square * square * inverse
    pulled = masses * inverse
    radial = square * (pulled + both[:, BLK:] * fifth)
    left = jnp.concatenate([*split2(radial), *split2(fifth)], axis=1)
    near, quad = weights[:, :BLK], weights[:, BLK:]
    none = jnp.zeros_like(near)
    right = jnp.concatenate(
        [
            jnp.concatenate([near, near, none, none], axis=1),
            jnp.concatenate([none, none, quad, quad], axis=1),
        ],
        axis=0,
    )
    return contract(left, right), pulled


def near_pair(targets, first, second, masses):
    weights = jnp.concatenate([first, second], axis=1)
    both = jnp.dot(targets, six(weights), preferred_element_type=F32)
    inverse = lax.rsqrt(both)
    pulled = masses * inverse
    radial = pulled * (inverse * inverse)
    left = jnp.concatenate([*split2(radial[:, :BLK]), *split2(radial[:, BLK:])], axis=1)
    right = jnp.concatenate([first, first, second, second], axis=1)
    return contract(left, right), pulled[:, :BLK] + pulled[:, BLK:]


def tall(masses):
    return jnp.concatenate([masses] * (BLK // 8), axis=0)


def force_kernel(
    cell_lists, near_lists, particles, cells, moved, neighbours, out,
    targets, cell_weights, cell_masses, near_weights, near_masses,
):
    blocks = cell_lists.shape[0]
    own_cells = cells.shape[1] // BLK
    peers, _, slots, _ = moved.shape

    def put_cell(slot, x, y, z, mass, xx, yy, xy, xz, yz):
        store_source(
            slot,
            cell_weights,
            jnp.concatenate(
                [distance_rows(x, y, z), quadrupole_rows(x, y, z, xx, yy, xy, xz, yz)], axis=1
            ),
        )
        cell_masses[slot] = mass

    def put_near(slot, x, y, z, mass):
        store_source(slot, near_weights, distance_rows(x, y, z))
        near_masses[slot] = mass

    def own_step(b, unused):
        columns = pl.ds(pl.multiple_of(b * BLK, BLK), BLK)
        put_cell(b, *(wide(cells[f : f + 1, columns]) for f in KEEP))
        return unused

    lax.fori_loop(0, own_cells, own_step, 0, unroll=2)

    def moved_step(s, unused):
        for k in range(slots):
            put_cell(
                own_cells + s * slots + k,
                *(wide(moved[s, f, k : k + 1, :]) for f in range(len(KEEP))),
            )
        return unused

    lax.fori_loop(0, peers, moved_step, 0)

    def target_step(j, unused):
        columns = pl.ds(pl.multiple_of(j * BLK, BLK), BLK)
        x, y, z, mass = (wide(particles[f : f + 1, columns]) for f in range(4))
        put_near(j, x, y, z, mass)
        high, middle, low = (v.astype(F32) for v in split3(target_rows(x, y, z)))
        pad = jnp.zeros((BLK - 6 * ROWS, BLK), F32)
        rows = jnp.concatenate([high, middle, low, high, middle, high, pad], axis=0)
        targets[j] = jnp.transpose(rows).astype(B16)
        return unused

    lax.fori_loop(0, blocks, target_step, 0)

    def neighbour_step(b, unused):
        put_near(blocks + b, *(wide(neighbours[b, f : f + 1, :]) for f in range(4)))
        return unused

    lax.fori_loop(0, neighbours.shape[0], neighbour_step, 0)

    def block_step(j, unused):
        columns = pl.ds(pl.multiple_of(j * BLK, BLK), BLK)
        mine = targets[j][:, : 6 * ROWS]

        def cell_step(l, carried):
            total, potential = carried
            b = cell_lists[j, l]
            sums, pulled = cell_pair(mine, cell_weights[b], tall(cell_masses[b]))
            return total + sums, potential + pulled

        def near_step(l, carried):
            total, potential = carried
            b, c = near_lists[j, 2 * l], near_lists[j, 2 * l + 1]
            masses = jnp.concatenate([tall(near_masses[b]), tall(near_masses[c])], axis=1)
            sums, pulled = near_pair(mine, near_weights[b], near_weights[c], masses)
            return total + sums, potential + pulled

        total = jnp.zeros((BLK, 6 * ROWS), F32)
        potential = jnp.zeros((BLK, BLK), F32)
        total, potential = lax.fori_loop(0, cell_lists.shape[1], cell_step, (total, potential), unroll=4)
        near_total = jnp.zeros((BLK, 3 * ROWS), F32)
        near_total, potential = lax.fori_loop(
            0, near_lists.shape[1] // 2, near_step, (near_total, potential), unroll=4
        )
        pad = jnp.zeros((BLK, BLK - 6 * ROWS), F32)
        sums = jnp.transpose(jnp.concatenate([total, pad], axis=1))
        near_sums = jnp.transpose(
            jnp.concatenate([near_total, jnp.zeros((BLK, BLK - 3 * ROWS), F32)], axis=1)
        )
        pulls = jnp.sum(jnp.transpose(potential), axis=0, keepdims=True)
        finish(particles, columns, sums, near_sums, pulls, out)
        return unused

    lax.fori_loop(0, blocks, block_step, 0)


def finish(particles, columns, sums, near_sums, pulls, out):
    x, y, z = (particles[f : f + 1, columns] for f in range(3))
    near = sums[0:16] + sums[16:32] + sums[32:48]
    near = near + near_sums[0:16] + near_sums[16:32] + near_sums[32:48]
    quad = sums[48:64] + sums[64:80] + sums[80:96]

    def row(values, i):
        return values[i : i + 1]

    whole = row(near, 10)
    qx, qy, qz, inner, xx, yy, zz, xy, xz, yz = (row(quad, i) for i in range(10))
    ax = xx * x + xy * y + xz * z
    ay = xy * x + yy * y + yz * z
    az = xz * x + yz * y + zz * z
    out[0:1, columns] = 0.4 * (ax - qx) - (x * whole - row(near, 0))
    out[1:2, columns] = 0.4 * (ay - qy) - (y * whole - row(near, 1))
    out[2:3, columns] = 0.4 * (az - qz) - (z * whole - row(near, 2))
    bent = ax * x + ay * y + az * z - 2 * (qx * x + qy * y + qz * z) + inner
    out[3:4, columns] = -pulls - 0.2 * bent


def exchange_cells(chosen):
    return lax.all_to_all(chosen, ("gx", "gy"), split_axis=0, concat_axis=0, tiled=True)


def body(particles, tree_cells, let_list, let_count, part_list, cell_lists, near_lists):
    part_blocks = jnp.transpose(particles.reshape(4, -1, BLK), (1, 0, 2))
    kept = jnp.concatenate([tree_cells[:6], tree_cells[7:]], axis=0)
    cell_blocks = jnp.transpose(kept.reshape(len(KEEP), -1, BLK), (1, 0, 2))
    peers = lax.axis_size(("gx", "gy"))
    slots = let_list.shape[2]
    live = lax.broadcasted_iota(jnp.int32, (peers, slots), 1) < let_count[0][:, None]
    chosen = jnp.where(live[:, :, None, None], cell_blocks[let_list[0]], 0.0)
    moved = exchange_cells(jnp.transpose(chosen, (0, 2, 1, 3)))
    near_parts = []
    for position, offset in enumerate(near_offsets):
        picked = part_blocks[part_list[0, position]]
        near_parts.append(from_behind(picked, ("gx", "gy"), offset))
    neighbours = jnp.concatenate(near_parts, axis=0)

    blocks = cell_lists.shape[0]
    pool = tree_cells.shape[1] // BLK + peers * slots
    near_pool = blocks + neighbours.shape[0]
    smem = pl.BlockSpec(memory_space=pltpu.SMEM)
    vmem = pl.BlockSpec(memory_space=pltpu.VMEM)
    return pl.pallas_call(
        force_kernel,
        out_shape=jax.ShapeDtypeStruct(particles.shape, F32),
        in_specs=[smem, smem, vmem, vmem, vmem, vmem],
        out_specs=vmem,
        scratch_shapes=[
            pltpu.VMEM((blocks, BLK, BLK), B16),
            pltpu.VMEM((pool, 3 * ROWS, 2 * BLK), B16),
            pltpu.VMEM((pool, 8, BLK), F32),
            pltpu.VMEM((near_pool, 3 * ROWS, BLK), B16),
            pltpu.VMEM((near_pool, 8, BLK), F32),
        ],
        compiler_params=pltpu.CompilerParams(vmem_limit_bytes=48 * 2**20),
    )(cell_lists, near_lists, particles, tree_cells, moved, neighbours)


def solution(mesh):
    return jax.shard_map(
        body,
        mesh=mesh,
        in_specs=(
            P(None, ("gx", "gy")),
            P(None, ("gx", "gy")),
            P(("gx", "gy"), None, None),
            P(("gx", "gy"), None),
            P(("gx", "gy"), None, None),
            P(("gx", "gy"), None),
            P(("gx", "gy"), None),
        ),
        out_specs=P(None, ("gx", "gy")),
        check_vma=False,
    )
```

time: 122 us -> 92.7 us (0.76)
  the two profiles are of different devices: /device:TPU:0 before, /device:TPU:8 now
where the time goes in v1:
time: 92.7 us; the launch traced here: 92.4 us
  Pallas kernels  60.2 us (65%)
  starting transfers between devices  19 us (20%)
  local copies, waits for them, and re-layouts  6.79 us (7%)
  waiting for transfers between devices  4.75 us (5%)
  other arithmetic  1.31 us (1%)
    pallas_call x1, Pallas kernels, body(): pl.pallas_call(force_kernel, out_shape=jax.ShapeDtypeStruct(particles.sha...  60.2 us
    ppermute x4, starting transfers between devices, from_behind(): return lax.ppermute(block, axis, route)  13 us
    all_to_all x1, starting transfers between devices, exchange_cells(): lax.all_to_all(chosen, ('gx', 'gy'), split_axis=0, concat_axis=0, tiled=T...  6.04 us
    ppermute x4, waiting for transfers between devices, from_behind(): return lax.ppermute(block, axis, route)  4.74 us
    gather x4, local copies, waits for them, and re-layouts, body(): picked = part_blocks[part_list[0, position]]  2.29 us
    slice x3, local copies, waits for them, and re-layouts, body(): kept = jnp.concatenate([tree_cells[:6], tree_cells[7:]], axis=0)  2.02 us
  transfers between devices with their start and end apart: 5, of which 1 were waited for; matrix products, arithmetic and copies ran while one was open for 3% of the time, Pallas kernels for 0%

profile of v1, /device:TPU:8, one launch (start us, length us, event | category | flops | bytes accessed | tf_op | source)
XLA Modules:
  0.0 92.4 jit_solution(9490908690584456540)
XLA Ops:
  0.0 1.1 %slice.19 = f32[3,8192]{1,0:T(4,128)S(1)} slice(f32[10,8192]{1,0:T(8,128)} %cells.1), slice={[7:10], [0:8192]} | slice | bytes 196608 | tf_op jit(solution)/shard_map/slice | solution.py:251
  1.1 0.0 slice-start
  1.1 0.9 %slice-done = f32[6,8192]{1,0:T(8,128)S(1)} async-done(((f32[10,8192]{1,0:T(8,128)}), f32[6,8192]{1,0:T(8,128)S(1)}, s32[]{:S(2)}) %slice-start) | async-done | bytes 196632 | tf_op jit(solution)/shard_map/slice | solution.py:251
  2.0 0.1 pad_maximum_fusion
  2.1 0.1 copy.21
  2.2 0.0 copy-start.4
  2.3 0.2 copy.26
  2.5 0.5 copy-done.4
  2.9 0.1 copy.15
  3.0 0.1 reshape.172
  3.1 0.0 copy-start.6
  3.2 0.6 copy-done.6
  3.8 0.1 iota_compare_fusion
  3.9 0.8 gather_fusion
  4.6 1.1 %fusion = f32[32,9,4,128]{3,2,1,0:T(4,128)} fusion(f32[32,4,9,128]{3,2,1,0:T(8,128)S(1)} %bitcast.38, pred[32,4]{1,0:T(8,128)(4,1)S(1)} %iota_compare_fusion), kind=kLoop, calls=%fused_computation.6 | loop fusion | flops 147456 | bytes 1179776 | tf_op jit(solution)/shard_map/jit(_where)/select_n | solution.py:256
  5.8 0.0 copy-start.5
  5.8 0.0 copy-start.1
  5.8 0.0 copy-start
  5.8 6.0 %all-to-all-start = ((f32[32,9,4,128]{3,2,1,0:T(4,128)}), f32[32,9,4,128]{3,2,1,0:T(4,128)S(1)}, u32[]{:S(2)}, u32[]{:S(2)}) async-start(f32[32,9,4,128]{3,2,1,0:T(4,128)} %fusion), calls=%async_computation | async-start | bytes 1179648 | tf_op jit(solution)/shard_map/all_to_all | solution.py:246
  11.8 0.0 copy-done.5
  11.9 0.0 copy-done.1
  11.9 0.6 gather_fusion.4
  12.4 4.3 %collective-permute-start.3 = (f32[4,4,128]{2,1,0:T(4,128)S(1)}, f32[4,4,128]{2,1,0:T(4,128)S(1)}, u32[]{:S(2)}, u32[]{:S(2)}) collective-permute-start(f32[4,4,128]{2,1,0:T(4,128)S(1)} %gather_fusion.4), channel_id=1, source_target_pairs={{2,0},{3,1},{4,2},{5,3},{6,4},{7,5},{8,6},{9,7},{10,8},{11,9},{12,... | collective-permute-start | bytes 24584 | tf_op jit(solution)/shard_map/ppermute | solution.py:23
  16.7 0.6 gather_fusion.3
  17.3 1.9 %collective-permute-start.2 = (f32[4,4,128]{2,1,0:T(4,128)S(1)}, f32[4,4,128]{2,1,0:T(4,128)S(1)}, u32[]{:S(2)}, u32[]{:S(2)}) collective-permute-start(f32[4,4,128]{2,1,0:T(4,128)S(1)} %gather_fusion.3), channel_id=1, source_target_pairs={{0,2},{1,3},{2,4},{3,5},{4,6},{5,7},{6,8},{7,9},{8,10},{9,11},{10,... | collective-permute-start | bytes 24584 | tf_op jit(solution)/shard_map/ppermute | solution.py:23
  19.2 0.6 gather_fusion.2
  19.8 4.9 %collective-permute-start.1 = (f32[4,4,128]{2,1,0:T(4,128)S(1)}, f32[4,4,128]{2,1,0:T(4,128)S(1)}, u32[]{:S(2)}, u32[]{:S(2)}) collective-permute-start(f32[4,4,128]{2,1,0:T(4,128)S(1)} %gather_fusion.2), channel_id=1, source_target_pairs={{1,0},{2,1},{3,2},{4,3},{5,4},{6,5},{7,6},{8,7},{9,8},{10,9},{11,1... | collective-permute-start | bytes 24584 | tf_op jit(solution)/shard_map/ppermute | solution.py:23
  24.7 0.0 copy-start.3
  24.7 0.6 gather_fusion.1
  25.3 1.9 %collective-permute-start = (f32[4,4,128]{2,1,0:T(4,128)S(1)}, f32[4,4,128]{2,1,0:T(4,128)S(1)}, u32[]{:S(2)}, u32[]{:S(2)}) collective-permute-start(f32[4,4,128]{2,1,0:T(4,128)S(1)} %gather_fusion.1), channel_id=1, source_target_pairs={{0,1},{1,2},{2,3},{3,4},{4,5},{5,6},{6,7},{7,8},{8,9},{9,10},{10,1... | collective-permute-start | bytes 24584 | tf_op jit(solution)/shard_map/ppermute | solution.py:23
  27.2 0.0 copy-done.3
  27.3 0.1 copy.18.near_lists
  27.3 0.0 copy-start.2
  27.3 0.0 collective-permute-done.3
  27.3 0.0 collective-permute-done.2
  27.3 0.0 collective-permute-done.1
  27.3 4.7 %collective-permute-done = f32[4,4,128]{2,1,0:T(4,128)S(1)} collective-permute-done((f32[4,4,128]{2,1,0:T(4,128)S(1)}, f32[4,4,128]{2,1,0:T(4,128)S(1)}, u32[]{:S(2)}, u32[]{:S(2)}) %collective-permute-start) | collective-permute-done | bytes 8224 | tf_op jit(solution)/shard_map/ppermute | solution.py:23
  32.1 0.0 all-to-all-done.moved
  32.1 0.0 copy-done
  32.1 0.0 copy-done.2
  32.1 60.2 %shard_map.73 = f32[4,2048]{1,0:T(4,128)} custom-call(s32[16,16]{1,0:T(8,128)S(1)} %copy-done.2, s32[16,8]{1,0:T(8,128)S(1)} %copy.18.near_lists, f32[4,2048]{1,0:T(4,128)S(1)} %copy-done.1, f32[10,8192]{1,0:T(8,128)S(1)} %copy-done, f32[32,9,4,128]{3,2,1,0:T(4,128)S(1)} %all-to-all-done.moved, f32[16,4,128]{2,1,0:T(4,128)S(1)} %pad_maximum_fusion.1.neighbours), custom_call_target="tpu_custom_call" | custom-call | tf_op jit(solution)/shard_map/pallas_call | solution.py:269
  (9 shorter events, 0.1 us)
Async XLA Ops:
  1.1 1.0 %slice-start = ((f32[10,8192]{1,0:T(8,128)}), f32[6,8192]{1,0:T(8,128)S(1)}, s32[]{:S(2)}) async-start(f32[10,8192]{1,0:T(8,128)} %cells.1), calls=%async_computation.1 | async-start | bytes 524288 | tf_op jit(solution)/shard_map/slice | solution.py:251
  2.2 0.7 copy-start.4
  3.1 0.7 copy-start.6
  5.8 6.1 %copy-start.5 = (s32[1,4,4]{2,1,0:T(4,128)S(1)}, s32[1,4,4]{2,1,0:T(4,128)}, u32[]{:S(2)}) copy-start(s32[1,4,4]{2,1,0:T(4,128)} %param.11) | copy-start | bytes 196
  5.8 6.1 %copy-start.1 = (f32[4,2048]{1,0:T(4,128)S(1)}, f32[4,2048]{1,0:T(4,128)}, u32[]{:S(2)}) copy-start(f32[4,2048]{1,0:T(4,128)} %particles.1) | copy-start | bytes 98308
  5.8 26.3 %copy-start = (f32[10,8192]{1,0:T(8,128)S(1)}, f32[10,8192]{1,0:T(8,128)}, u32[]{:S(2)}) copy-start(f32[10,8192]{1,0:T(8,128)} %cells.1) | copy-start | bytes 983044
  5.8 26.3 %all-to-all-start = ((f32[32,9,4,128]{3,2,1,0:T(4,128)}), f32[32,9,4,128]{3,2,1,0:T(4,128)S(1)}, u32[]{:S(2)}, u32[]{:S(2)}) async-start(f32[32,9,4,128]{3,2,1,0:T(4,128)} %fusion), calls=%async_computation | async-start | bytes 1179648 | tf_op jit(solution)/shard_map/all_to_all | solution.py:246
  12.4 14.9 %collective-permute-start.3 = (f32[4,4,128]{2,1,0:T(4,128)S(1)}, f32[4,4,128]{2,1,0:T(4,128)S(1)}, u32[]{:S(2)}, u32[]{:S(2)}) collective-permute-start(f32[4,4,128]{2,1,0:T(4,128)S(1)} %gather_fusion.4), channel_id=1, source_target_pairs={{2,0},{3,1},{4,2},{5,3},{6,4},{7,5},{8,6},{9,7},{10,8},{11,9},{12,... | collective-permute-start | bytes 24584 | tf_op jit(solution)/shard_map/ppermute | solution.py:23
  17.3 10.0 %collective-permute-start.2 = (f32[4,4,128]{2,1,0:T(4,128)S(1)}, f32[4,4,128]{2,1,0:T(4,128)S(1)}, u32[]{:S(2)}, u32[]{:S(2)}) collective-permute-start(f32[4,4,128]{2,1,0:T(4,128)S(1)} %gather_fusion.3), channel_id=1, source_target_pairs={{0,2},{1,3},{2,4},{3,5},{4,6},{5,7},{6,8},{7,9},{8,10},{9,11},{10,... | collective-permute-start | bytes 24584 | tf_op jit(solution)/shard_map/ppermute | solution.py:23
  19.8 7.5 %collective-permute-start.1 = (f32[4,4,128]{2,1,0:T(4,128)S(1)}, f32[4,4,128]{2,1,0:T(4,128)S(1)}, u32[]{:S(2)}, u32[]{:S(2)}) collective-permute-start(f32[4,4,128]{2,1,0:T(4,128)S(1)} %gather_fusion.2), channel_id=1, source_target_pairs={{1,0},{2,1},{3,2},{4,3},{5,4},{6,5},{7,6},{8,7},{9,8},{10,9},{11,1... | collective-permute-start | bytes 24584 | tf_op jit(solution)/shard_map/ppermute | solution.py:23
  24.7 2.5 %copy-start.3 = (s32[16,8]{0,1:T(8,128)S(1)}, s32[16,8]{0,1:T(8,128)}, u32[]{:S(2)}) copy-start(s32[16,8]{0,1:T(8,128)} %param.13) | copy-start | bytes 1540
  25.3 6.8 %collective-permute-start = (f32[4,4,128]{2,1,0:T(4,128)S(1)}, f32[4,4,128]{2,1,0:T(4,128)S(1)}, u32[]{:S(2)}, u32[]{:S(2)}) collective-permute-start(f32[4,4,128]{2,1,0:T(4,128)S(1)} %gather_fusion.1), channel_id=1, source_target_pairs={{0,1},{1,2},{2,3},{3,4},{4,5},{5,6},{6,7},{7,8},{8,9},{9,10},{10,1... | collective-permute-start | bytes 24584 | tf_op jit(solution)/shard_map/ppermute | solution.py:23
  27.3 4.8 %copy-start.2 = (s32[16,16]{1,0:T(8,128)S(1)}, s32[16,16]{1,0:T(8,128)}, u32[]{:S(2)}) copy-start(s32[16,16]{1,0:T(8,128)} %cell_lists.1) | copy-start | bytes 3076

commit v2 on v0

v2 whole, which is shorter than its diff:
```python
import functools

import jax
import jax.numpy as jnp
from jax import lax
from jax.experimental import pallas as pl
from jax.experimental.pallas import tpu as pltpu
from jax.sharding import PartitionSpec as P

BLK = 128
ROWS = 16
SUMS = 4
SOFTENING = 0.0025
near_offsets = (1, -1, 2, -2)
F32 = jnp.float32
B16 = jnp.bfloat16


def from_behind(block, axis, distance):
    devices = range(lax.axis_size(axis))
    route = [(i - distance, i) for i in devices if i - distance in devices]
    return lax.ppermute(block, axis, route)


def at_block(index):
    return pl.ds(pl.multiple_of(index * BLK, BLK), BLK)


def split3(value):
    high = value.astype(B16)
    rest = value - high.astype(F32)
    middle = rest.astype(B16)
    low = (rest - middle.astype(F32)).astype(B16)
    return high, middle, low


def split2(value):
    high = value.astype(B16)
    return high, (value - high.astype(F32)).astype(B16)


def stack_rows(rows):
    sub = lax.broadcasted_iota(jnp.int32, (8, BLK), 0)
    out = rows[0]
    for i in range(1, len(rows)):
        out = jnp.where(sub == i, rows[i], out)
    return out


def wide(row):
    return jnp.broadcast_to(row, (8, BLK))


def quadrupole_rows(x, y, z, xx, yy, xy, xz, yz):
    xx, yy, xy, xz, yz = (2.5 * v for v in (xx, yy, xy, xz, yz))
    zz = -(xx + yy)
    qx = xx * x + xy * y + xz * z
    qy = xy * x + yy * y + yz * z
    qz = xz * x + yz * y + zz * z
    inner = qx * x + qy * y + qz * z
    first = stack_rows([qx, qy, qz, inner, xx, yy, zz, xy])
    second = stack_rows([jnp.zeros((8, BLK), F32), yz, xz])
    return jnp.concatenate([first, second], axis=0)


def target_rows(x, y, z):
    one = jnp.ones((8, BLK), F32)
    first = stack_rows([-2 * x, -2 * y, -2 * z, one, x * x, y * y, z * z, 2 * x * y])
    second = stack_rows([jnp.zeros((8, BLK), F32), 2 * y * z, 2 * x * z])
    return jnp.concatenate([first, second], axis=0)


def put_weights(weights, slot, rows):
    high, middle, low = split3(rows)
    weights[slot, 0:ROWS] = high
    weights[slot, ROWS : 2 * ROWS] = middle
    weights[slot, 2 * ROWS :] = low


def six(weights):
    high, middle, low = weights[0:ROWS], weights[ROWS : 2 * ROWS], weights[2 * ROWS :]
    return jnp.concatenate([high, high, high, middle, middle, low], axis=0)


def contract(left, right):
    return lax.dot_general(left, right, (((1,), (1,)), ((), ())), preferred_element_type=F32)


def pick_kernel(let_list, let_count, part_list, cells, particles, chosen, *picked):
    peers, slots = let_list.shape
    sub = lax.broadcasted_iota(jnp.int32, (4, BLK), 0)

    def peer_step(d, unused):
        count = let_count[0, d]
        for k in range(slots):
            columns = at_block(let_list[d, k])
            live = k < count
            chosen[d, k] = jnp.where(live, cells[0:4, columns], 0.0)
            quad = jnp.where(sub == 2, cells[8:9, columns], cells[4:8, columns])
            chosen[d, slots + k] = jnp.where(live, quad, 0.0)
            chosen[d, 2 * slots, k : k + 1, :] = jnp.where(live, cells[9:10, columns], 0.0)
        return unused

    lax.fori_loop(0, peers, peer_step, 0, unroll=2)
    for position, out in enumerate(picked):
        for k in range(part_list.shape[1]):
            out[k] = particles[:, at_block(part_list[position, k])]


def cell_group(size, j, first, lists, targets, spread, places, weights, sums, quads):
    blocks = [lists[j, first + i] for i in range(size)]
    coefficients = jnp.concatenate([six(weights[b]) for b in blocks], axis=1)
    bent = jnp.dot(targets[j], coefficients, preferred_element_type=F32)
    left = []
    for low in range(0, BLK, 16):
        rows = slice(low, low + 16)
        x, y, z = (spread[j, f, rows] for f in range(3))
        ax, ay, az, potential = (sums[j, f, rows] for f in range(SUMS))
        parts = []
        for i, b in enumerate(blocks):
            rx, ry, rz = x - places[b, 0:1, :], y - places[b, 1:2, :], z - places[b, 2:3, :]
            inverse = lax.rsqrt(rx * rx + ry * ry + (rz * rz + SOFTENING))
            square = inverse * inverse
            fifth = square * square * inverse
            pulled = inverse * places[b, 3:4, :]
            radial = square * (pulled + bent[rows, i * BLK : (i + 1) * BLK] * fifth)
            ax += radial * rx
            ay += radial * ry
            az += radial * rz
            potential += pulled
            parts += split2(fifth)
        for f, value in enumerate((ax, ay, az, potential)):
            sums[j, f, rows] = value
        left.append(jnp.concatenate(parts, axis=1))
    right = jnp.concatenate([weights[b] for b in blocks for _ in range(2)], axis=1)
    quads[j, :, : 3 * ROWS] += contract(jnp.concatenate(left, axis=0), right)


def near_group(size, j, first, lists, spread, places, sums):
    blocks = [lists[j, first + i] for i in range(size)]
    for low in range(0, BLK, 16):
        rows = slice(low, low + 16)
        x, y, z = (spread[j, f, rows] for f in range(3))
        ax, ay, az, potential = (sums[j, f, rows] for f in range(SUMS))
        for b in blocks:
            rx, ry, rz = x - places[b, 0:1, :], y - places[b, 1:2, :], z - places[b, 2:3, :]
            inverse = lax.rsqrt(rx * rx + ry * ry + (rz * rz + SOFTENING))
            pulled = inverse * places[b, 3:4, :]
            radial = pulled * (inverse * inverse)
            ax += radial * rx
            ay += radial * ry
            az += radial * rz
            potential += pulled
        for f, value in enumerate((ax, ay, az, potential)):
            sums[j, f, rows] = value


def in_groups(count, group):
    fours = (count + 1) // 4

    def four(i, unused):
        group(4, 4 * i)
        return unused

    lax.fori_loop(0, fours, four, 0)

    @pl.when(4 * fours < count)
    def _():
        group(2, 4 * fours)


def keep_some(j, source, target, wanted, nothing):
    count = jnp.int32(0)
    for l in range(source.shape[1]):
        slot, live = wanted(source[j, l])
        target[j, count] = slot
        count = count + live.astype(jnp.int32)
    for extra in range(3):
        target[j, count + extra] = nothing
    return count


def spread_targets(j, columns, spread):
    for f in range(3):
        spread[j, f] = jnp.broadcast_to(columns[j, :, f : f + 1], (BLK, BLK)) * (-0.5)


def clear(j, sums, quads):
    for f in range(SUMS):
        sums[j, f] = jnp.zeros((BLK, BLK), F32)
    quads[j] = jnp.zeros((BLK, BLK), F32)


def forces_of(j, particles, sums, quads):
    lane = lax.broadcasted_iota(jnp.int32, (BLK, BLK), 1)
    mixed = quads[j]
    for f in range(SUMS):
        mixed = jnp.where(lane == 64 + f, jnp.sum(sums[j, f], axis=1, keepdims=True), mixed)
    mixed = jnp.transpose(mixed)
    quad = mixed[0:16] + mixed[16:32] + mixed[32:48]
    qx, qy, qz, inner, xx, yy, zz, xy = (quad[i : i + 1] for i in range(8))
    yz, xz = quad[9:10], quad[10:11]
    sx, sy, sz, pulls = (mixed[64 + f : 65 + f] for f in range(SUMS))
    x, y, z = (particles[f : f + 1, at_block(j)] for f in range(3))
    ax = xx * x + xy * y + xz * z
    ay = xy * x + yy * y + yz * z
    az = xz * x + yz * y + zz * z
    bent = ax * x + ay * y + az * z - 2 * (qx * x + qy * y + qz * z) + inner
    return (
        0.4 * (ax - qx) - sx,
        0.4 * (ay - qy) - sy,
        0.4 * (az - qz) - sz,
        -pulls - 0.2 * bent,
    )


def own_kernel(
    cell_lists, near_lists, particles, cells, out, targets, columns,
    lists, near_kept, spread, places, weights, near_places, sums, quads,
):
    blocks = cell_lists.shape[0]
    own_cells = cells.shape[1] // BLK

    def prepare_cell(b, unused):
        x, y, z, _, xx, yy, _, xy, xz, yz = (wide(cells[f : f + 1, at_block(b)]) for f in range(10))
        put_weights(weights, b, quadrupole_rows(x, y, z, xx, yy, xy, xz, yz))
        places[b, 0:4, :] = cells[0:4, at_block(b)]
        return unused

    lax.fori_loop(0, own_cells, prepare_cell, 0, unroll=4)
    weights[own_cells] = jnp.zeros((3 * ROWS, BLK), B16)
    places[own_cells] = jnp.zeros((8, BLK), F32)
    near_places[blocks] = jnp.zeros((8, BLK), F32)

    def prepare_target(j, unused):
        near_places[j, 0:4, :] = particles[:, at_block(j)]
        x, y, z = (wide(particles[f : f + 1, at_block(j)]) for f in range(3))
        high, middle, low = (v.astype(F32) for v in split3(target_rows(x, y, z)))
        exact = target_rows(x, y, z)
        pad = jnp.zeros((BLK - 7 * ROWS, BLK), F32)
        rows = jnp.concatenate([high, middle, low, high, middle, high, exact, pad], axis=0)
        turned = jnp.transpose(rows)
        targets[j] = turned[:, : 6 * ROWS].astype(B16)
        columns[j] = turned[:, 6 * ROWS : 7 * ROWS]
        spread_targets(j, columns, spread)
        clear(j, sums, quads)
        return unused

    lax.fori_loop(0, blocks, prepare_target, 0)

    def block_step(j, unused):
        count = keep_some(j, cell_lists, lists, lambda b: (b, b < own_cells), own_cells)
        near_count = keep_some(j, near_lists, near_kept, lambda b: (b, b < blocks), blocks)
        in_groups(
            count,
            lambda size, first: cell_group(
                size, j, first, lists, targets, spread, places, weights, sums, quads
            ),
        )
        in_groups(
            near_count,
            lambda size, first: near_group(size, j, first, near_kept, spread, near_places, sums),
        )
        return unused

    lax.fori_loop(0, blocks, block_step, 0)

    def finish_step(j, unused):
        for f, row in enumerate(forces_of(j, particles, sums, quads)):
            out[f : f + 1, at_block(j)] = row
        return unused

    lax.fori_loop(0, blocks, finish_step, 0, unroll=2)


def moved_kernel(
    own_cells, cell_lists, near_lists, particles, targets, columns, partial, moved, *rest
):
    neighbours, (out, counts, lists, near_kept, spread, places, weights, near_places, sums, quads) = (
        rest[:-10], rest[-10:],
    )
    blocks = cell_lists.shape[0]
    peers, slots = moved.shape[0], moved.shape[2]
    near_moved = len(neighbours) * neighbours[0].shape[0]

    def prepare_peer(s, unused):
        alive = jnp.zeros((4, BLK), jnp.int32)
        for k in range(slots):
            b = s * slots + k
            x, y, z = (wide(moved[s, k, f : f + 1, :]) for f in range(3))
            xx, yy, xz, xy = (wide(moved[s, slots + k, f : f + 1, :]) for f in range(4))
            yz = wide(moved[s, 2 * slots, k : k + 1, :])
            put_weights(weights, b, quadrupole_rows(x, y, z, xx, yy, xy, xz, yz))
            places[b, 0:4, :] = moved[s, k]
            some = jnp.abs(moved[s, k]) + jnp.abs(moved[s, slots + k])
            some = some + jnp.abs(moved[s, 2 * slots, k : k + 1, :])
            alive = jnp.where(some > 0, k + 1, alive)
        counts[s] = jnp.max(alive)
        return unused

    lax.fori_loop(0, peers, prepare_peer, 0)
    weights[peers * slots] = jnp.zeros((3 * ROWS, BLK), B16)
    places[peers * slots] = jnp.zeros((8, BLK), F32)
    for i, block in enumerate(neighbours):
        for k in range(block.shape[0]):
            near_places[i * block.shape[0] + k, 0:4, :] = block[k]
    near_places[near_moved] = jnp.zeros((8, BLK), F32)

    def prepare_target(j, unused):
        spread_targets(j, columns, spread)
        clear(j, sums, quads)
        return unused

    lax.fori_loop(0, blocks, prepare_target, 0)

    def wanted(b):
        slot = jnp.maximum(b - own_cells, 0)
        live = (b >= own_cells) & (slot % slots < counts[slot // slots])
        return slot, live

    def block_step(j, unused):
        count = keep_some(j, cell_lists, lists, wanted, peers * slots)
        near_count = keep_some(
            j, near_lists, near_kept, lambda b: (b - blocks, b >= blocks), near_moved
        )
        in_groups(
            count,
            lambda size, first: cell_group(
                size, j, first, lists, targets, spread, places, weights, sums, quads
            ),
        )
        in_groups(
            near_count,
            lambda size, first: near_group(size, j, first, near_kept, spread, near_places, sums),
        )
        return unused

    lax.fori_loop(0, blocks, block_step, 0)

    def finish_step(j, unused):
        for f, row in enumerate(forces_of(j, particles, sums, quads)):
            out[f : f + 1, at_block(j)] = row + partial[f : f + 1, at_block(j)]
        return unused

    lax.fori_loop(0, blocks, finish_step, 0, unroll=2)


def scratch(blocks, cells, near, list_width, near_width):
    return [
        pltpu.SMEM((blocks, list_width + 4), jnp.int32),
        pltpu.SMEM((blocks, near_width + 4), jnp.int32),
        pltpu.VMEM((blocks, 3, BLK, BLK), F32),
        pltpu.VMEM((cells + 1, 8, BLK), F32),
        pltpu.VMEM((cells + 1, 3 * ROWS, BLK), B16),
        pltpu.VMEM((near + 1, 8, BLK), F32),
        pltpu.VMEM((blocks, SUMS, BLK, BLK), F32),
        pltpu.VMEM((blocks, BLK, BLK), F32),
    ]


def body(particles, tree_cells, let_list, let_count, part_list, cell_lists, near_lists):
    peers = lax.axis_size(("gx", "gy"))
    slots = let_list.shape[2]
    near_slots = part_list.shape[2]
    blocks, list_width = cell_lists.shape
    near_width = near_lists.shape[1]
    own_cells = tree_cells.shape[1] // BLK
    smem = pl.BlockSpec(memory_space=pltpu.SMEM)
    vmem = pl.BlockSpec(memory_space=pltpu.VMEM)
    params = pltpu.CompilerParams(vmem_limit_bytes=48 * 2**20)

    chosen, *picked = pl.pallas_call(
        pick_kernel,
        out_shape=[jax.ShapeDtypeStruct((peers, 2 * slots + 1, 4, BLK), F32)]
        + [jax.ShapeDtypeStruct((near_slots, 4, BLK), F32) for _ in near_offsets],
        in_specs=[smem, smem, smem, vmem, vmem],
        out_specs=[vmem] * (1 + len(near_offsets)),
        compiler_params=params,
    )(let_list[0], let_count, part_list[0], tree_cells, particles)
    moved = lax.all_to_all(chosen, ("gx", "gy"), split_axis=0, concat_axis=0, tiled=True)
    neighbours = [
        from_behind(block, ("gx", "gy"), offset) for block, offset in zip(picked, near_offsets)
    ]

    partial, targets, columns = pl.pallas_call(
        own_kernel,
        out_shape=[
            jax.ShapeDtypeStruct(particles.shape, F32),
            jax.ShapeDtypeStruct((blocks, BLK, 6 * ROWS), B16),
            jax.ShapeDtypeStruct((blocks, BLK, ROWS), F32),
        ],
        in_specs=[smem, smem, vmem, vmem],
        out_specs=[vmem] * 3,
        scratch_shapes=scratch(blocks, own_cells, blocks, list_width, near_width),
        compiler_params=params,
        cost_estimate=pl.CostEstimate(flops=10**9, bytes_accessed=10**6, transcendentals=10**6),
    )(cell_lists, near_lists, particles, tree_cells)

    near_moved = len(neighbours) * near_slots
    return pl.pallas_call(
        functools.partial(moved_kernel, own_cells),
        out_shape=jax.ShapeDtypeStruct(particles.shape, F32),
        in_specs=[smem, smem] + [vmem] * (5 + len(neighbours)),
        out_specs=vmem,
        scratch_shapes=[pltpu.SMEM((peers,), jnp.int32)]
        + scratch(blocks, peers * slots, near_moved, list_width, near_width),
        compiler_params=params,
    )(cell_lists, near_lists, particles, targets, columns, partial, moved, *neighbours)


def solution(mesh):
    return jax.shard_map(
        body,
        mesh=mesh,
        in_specs=(
            P(None, ("gx", "gy")),
            P(None, ("gx", "gy")),
            P(("gx", "gy"), None, None),
            P(("gx", "gy"), None),
            P(("gx", "gy"), None, None),
            P(("gx", "gy"), None),
            P(("gx", "gy"), None),
        ),
        out_specs=P(None, ("gx", "gy")),
        check_vma=False,
    )
```

time: 122 us -> 79.4 us (0.65)
  the two profiles are of different devices: /device:TPU:0 before, /device:TPU:8 now
where the time goes in v2:
time: 79.4 us; the launch traced here: 79.6 us
  Pallas kernels  55.1 us (69%)
  starting transfers between devices  21 us (26%)
  local copies, waits for them, and re-layouts  3.32 us (4%)
    pallas_call x1, Pallas kernels, body(): pl.pallas_call(functools.partial(moved_kernel, own_cells), out_shape=jax....  30.7 us
    pallas_call x1, Pallas kernels, body(): pl.pallas_call(own_kernel, out_shape=[jax.ShapeDtypeStruct(particles.shap...  22.1 us
    ppermute x4, starting transfers between devices, from_behind(): return lax.ppermute(block, axis, route)  15 us
    all_to_all x1, starting transfers between devices, body(): lax.all_to_all(chosen, ('gx', 'gy'), split_axis=0, concat_axis=0, tiled=T...  6.04 us
    unnamed x17, local copies, waits for them, and re-layouts  2.55 us
    pallas_call x1, Pallas kernels, body(): pl.pallas_call(pick_kernel, out_shape=[jax.ShapeDtypeStruct((peers, 2 * s...  2.17 us
  transfers between devices with their start and end apart: 5, of which 0 were waited for; matrix products, arithmetic and copies ran while one was open for 0% of the time, Pallas kernels for 28%

profile of v2, /device:TPU:8, one launch (start us, length us, event | category | flops | bytes accessed | tf_op | source)
XLA Modules:
  0.0 79.6 jit_solution(3643109089445949128)
XLA Ops:
  0.0 0.0 copy-start.5
  0.0 0.8 copy.9.let_list
  0.8 0.0 copy-start.6
  0.8 0.0 copy-done.5
  0.8 0.7 copy-done.6
  1.4 0.0 copy-start
  1.4 1.0 %copy-done = f32[10,8192]{1,0:T(8,128)S(1)} copy-done((f32[10,8192]{1,0:T(8,128)S(1)}, f32[10,8192]{1,0:T(8,128)}, u32[]{:S(2)}) %copy-start) | copy-done | bytes 327704
  2.5 0.0 copy-start.2
  2.5 0.8 copy-done.2
  3.2 2.2 %shard_map.74 = (f32[32,9,4,128]{3,2,1,0:T(4,128)}, f32[4,4,128]{2,1,0:T(4,128)S(1)}, f32[4,4,128]{2,1,0:T(4,128)S(1)}, f32[4,4,128]{2,1,0:T(4,128)S(1)}, f32[4,4,128]{2,1,0:T(4,128)S(1)}) custom-call(s32[32,4]{1,0:T(8,128)S(1)} %copy.9.let_list, s32[1,32]{1,0:T(1,128)S(1)} %copy-done.6, s32[4,4]{1,0:T(4,128)S(1)} %bitcast.2, f32[10,8192]{1,0:T(8,128)S(1)} %copy-done, ...), custom_call_target="tpu_custom_call" | custom-call | tf_op jit(solution)/shard_map/pallas_call | solution.py:372
  5.4 0.0 copy-start.1
  5.4 0.0 copy-start.3
  5.4 6.0 %all-to-all-start = ((f32[32,9,4,128]{3,2,1,0:T(4,128)}), f32[32,9,4,128]{3,2,1,0:T(4,128)S(1)}, u32[]{:S(2)}, u32[]{:S(2)}) async-start(f32[32,9,4,128]{3,2,1,0:T(4,128)} %get-tuple-element.16), calls=%async_computation | async-start | bytes 1179648 | tf_op jit(solution)/shard_map/all_to_all | solution.py:380
  11.5 0.0 copy-start.7
  11.5 2.1 %collective-permute-start = (f32[4,4,128]{2,1,0:T(4,128)S(1)}, f32[4,4,128]{2,1,0:T(4,128)S(1)}, u32[]{:S(2)}, u32[]{:S(2)}) collective-permute-start(f32[4,4,128]{2,1,0:T(4,128)S(1)} %get-tuple-element.17), channel_id=1, source_target_pairs={{0,1},{1,2},{2,3},{3,4},{4,5},{5,6},{6,7},{7,8},{8,9},{9,10},{10,1... | collective-permute-start | bytes 24584 | tf_op jit(solution)/shard_map/ppermute | solution.py:22
  13.5 0.0 copy-start.4
  13.6 5.3 %collective-permute-start.1 = (f32[4,4,128]{2,1,0:T(4,128)S(1)}, f32[4,4,128]{2,1,0:T(4,128)S(1)}, u32[]{:S(2)}, u32[]{:S(2)}) collective-permute-start(f32[4,4,128]{2,1,0:T(4,128)S(1)} %get-tuple-element.18), channel_id=1, source_target_pairs={{1,0},{2,1},{3,2},{4,3},{5,4},{6,5},{7,6},{8,7},{9,8},{10,9},{11,1... | collective-permute-start | bytes 24584 | tf_op jit(solution)/shard_map/ppermute | solution.py:22
  18.9 1.9 %collective-permute-start.2 = (f32[4,4,128]{2,1,0:T(4,128)S(1)}, f32[4,4,128]{2,1,0:T(4,128)S(1)}, u32[]{:S(2)}, u32[]{:S(2)}) collective-permute-start(f32[4,4,128]{2,1,0:T(4,128)S(1)} %get-tuple-element.19), channel_id=1, source_target_pairs={{0,2},{1,3},{2,4},{3,5},{4,6},{5,7},{6,8},{7,9},{8,10},{9,11},{10,... | collective-permute-start | bytes 24584 | tf_op jit(solution)/shard_map/ppermute | solution.py:22
  20.8 5.7 %collective-permute-start.3 = (f32[4,4,128]{2,1,0:T(4,128)S(1)}, f32[4,4,128]{2,1,0:T(4,128)S(1)}, u32[]{:S(2)}, u32[]{:S(2)}) collective-permute-start(f32[4,4,128]{2,1,0:T(4,128)S(1)} %get-tuple-element.20), channel_id=1, source_target_pairs={{2,0},{3,1},{4,2},{5,3},{6,4},{7,5},{8,6},{9,7},{10,8},{11,9},{12,... | collective-permute-start | bytes 24584 | tf_op jit(solution)/shard_map/ppermute | solution.py:22
  26.5 0.0 copy-done.7
  26.5 0.1 copy.10.near_lists
  26.6 0.0 copy-done.1
  26.6 0.0 copy-done.3
  26.6 0.0 copy-done.4
  26.6 22.1 %shard_map.73 = (f32[4,2048]{1,0:T(4,128)S(1)}, bf16[16,128,96]{2,1,0:T(8,128)(2,1)S(1)}, f32[16,128,16]{2,1,0:T(8,128)S(1)}) custom-call(s32[16,16]{1,0:T(8,128)S(1)} %copy-done.4, s32[16,8]{1,0:T(8,128)S(1)} %copy.10.near_lists, f32[4,2048]{1,0:T(4,128)S(1)} %copy-done.3, f32[10,8192]{1,0:T(8,128)S(1)} %copy-done.1), custom_call_target="tpu_custom_call" | custom-call | flops 1000000000 | bytes 1000000 | tf_op jit(solution)/shard_map/pallas_call | solution.py:385
  48.8 0.0 collective-permute-done.rest_0_
  48.8 0.0 collective-permute-done.1.rest_1_
  48.8 0.0 collective-permute-done.2.rest_2_
  48.8 0.0 collective-permute-done.3.rest_3_
  48.8 0.0 all-to-all-done.moved
  48.8 30.7 %shard_map.75 = f32[4,2048]{1,0:T(4,128)} custom-call(s32[16,16]{1,0:T(8,128)S(1)} %copy-done.4, s32[16,8]{1,0:T(8,128)S(1)} %copy.10.near_lists, f32[4,2048]{1,0:T(4,128)S(1)} %copy-done.3, bf16[16,128,96]{2,1,0:T(8,128)(2,1)S(1)} %get-tuple-element.13.targets, f32[16,128,16]{2,1,0:T(8,128)S(1)} %get-tuple-element.14.columns, ...), custom_call_target="tpu_custom_call" | custom-call | tf_op jit(solution)/shard_map/pallas_call | solution.py:400
Async XLA Ops:
  0.0 0.8 copy-start.5
  0.8 0.7 copy-start.6
  1.4 1.0 %copy-start = (f32[10,8192]{1,0:T(8,128)S(1)}, f32[10,8192]{1,0:T(8,128)}, u32[]{:S(2)}) copy-start(f32[10,8192]{1,0:T(8,128)} %cells.3) | copy-start | bytes 983044
  2.5 0.8 copy-start.2
  5.4 21.2 %copy-start.1 = (f32[10,8192]{1,0:T(8,128)S(1)}, f32[10,8192]{1,0:T(8,128)}, u32[]{:S(2)}) copy-start(f32[10,8192]{1,0:T(8,128)} %cells.3) | copy-start | bytes 983044
  5.4 21.2 %copy-start.3 = (f32[4,2048]{1,0:T(4,128)S(1)}, f32[4,2048]{1,0:T(4,128)}, u32[]{:S(2)}) copy-start(f32[4,2048]{1,0:T(4,128)} %particles.5) | copy-start | bytes 98308
  5.4 43.4 %all-to-all-start = ((f32[32,9,4,128]{3,2,1,0:T(4,128)}), f32[32,9,4,128]{3,2,1,0:T(4,128)S(1)}, u32[]{:S(2)}, u32[]{:S(2)}) async-start(f32[32,9,4,128]{3,2,1,0:T(4,128)} %get-tuple-element.16), calls=%async_computation | async-start | bytes 1179648 | tf_op jit(solution)/shard_map/all_to_all | solution.py:380
  11.5 15.1 %copy-start.7 = (s32[16,8]{0,1:T(8,128)S(1)}, s32[16,8]{0,1:T(8,128)}, u32[]{:S(2)}) copy-start(s32[16,8]{0,1:T(8,128)} %param.13) | copy-start | bytes 1540
  11.5 37.3 %collective-permute-start = (f32[4,4,128]{2,1,0:T(4,128)S(1)}, f32[4,4,128]{2,1,0:T(4,128)S(1)}, u32[]{:S(2)}, u32[]{:S(2)}) collective-permute-start(f32[4,4,128]{2,1,0:T(4,128)S(1)} %get-tuple-element.17), channel_id=1, source_target_pairs={{0,1},{1,2},{2,3},{3,4},{4,5},{5,6},{6,7},{7,8},{8,9},{9,10},{10,1... | collective-permute-start | bytes 24584 | tf_op jit(solution)/shard_map/ppermute | solution.py:22
  13.5 13.1 %copy-start.4 = (s32[16,16]{1,0:T(8,128)S(1)}, s32[16,16]{1,0:T(8,128)}, u32[]{:S(2)}) copy-start(s32[16,16]{1,0:T(8,128)} %cell_lists.3) | copy-start | bytes 3076
  13.6 35.2 %collective-permute-start.1 = (f32[4,4,128]{2,1,0:T(4,128)S(1)}, f32[4,4,128]{2,1,0:T(4,128)S(1)}, u32[]{:S(2)}, u32[]{:S(2)}) collective-permute-start(f32[4,4,128]{2,1,0:T(4,128)S(1)} %get-tuple-element.18), channel_id=1, source_target_pairs={{1,0},{2,1},{3,2},{4,3},{5,4},{6,5},{7,6},{8,7},{9,8},{10,9},{11,1... | collective-permute-start | bytes 24584 | tf_op jit(solution)/shard_map/ppermute | solution.py:22
  18.9 29.9 %collective-permute-start.2 = (f32[4,4,128]{2,1,0:T(4,128)S(1)}, f32[4,4,128]{2,1,0:T(4,128)S(1)}, u32[]{:S(2)}, u32[]{:S(2)}) collective-permute-start(f32[4,4,128]{2,1,0:T(4,128)S(1)} %get-tuple-element.19), channel_id=1, source_target_pairs={{0,2},{1,3},{2,4},{3,5},{4,6},{5,7},{6,8},{7,9},{8,10},{9,11},{10,... | collective-permute-start | bytes 24584 | tf_op jit(solution)/shard_map/ppermute | solution.py:22
  20.8 28.0 %collective-permute-start.3 = (f32[4,4,128]{2,1,0:T(4,128)S(1)}, f32[4,4,128]{2,1,0:T(4,128)S(1)}, u32[]{:S(2)}, u32[]{:S(2)}) collective-permute-start(f32[4,4,128]{2,1,0:T(4,128)S(1)} %get-tuple-element.20), channel_id=1, source_target_pairs={{2,0},{3,1},{4,2},{5,3},{6,4},{7,5},{8,6},{9,7},{10,8},{11,9},{12,... | collective-permute-start | bytes 24584 | tf_op jit(solution)/shard_map/ppermute | solution.py:22
